TPU v7x, 256 devices: a whole 4x4x8 slice. The times are simulated.
256 devices in a mesh: fsdp: 8 (over y, core), tp: 16 (over x_lo, z), layer: 2 (over x_hi).
Axes of the slice: x: 4 (x_hi: 2, x_lo: 2; x = x_hi * 2 + x_lo), y: 4, z: 8, core: 2. Of those that a mesh axis runs over, the one named last changes fastest.
Arguments:
- gradient: bfloat16 [8192, 14336], P('fsdp', ('tp', 'layer')), may hold values from -6 to 6
- left_basis: bfloat16 [8192, 8192], P('fsdp', ('tp', 'layer')), may hold values from -0.0625 to 0.0625
- first_moment: float32 [8192, 14336], P('fsdp', ('tp', 'layer')), may hold values from -4 to 4
- second_moment: float32 [8192, 14336], P('fsdp', ('tp', 'layer')), may hold values from 0.05 to 5
Outputs:
- update: bfloat16 [8192, 14336], P('fsdp', ('tp', 'layer'))
- first_new: float32 [8192, 14336], P('fsdp', ('tp', 'layer'))
- second_new: float32 [8192, 14336], P('fsdp', ('tp', 'layer'))
All inputs are finite; a program needn't handle non-finite values.
Results may differ from a plain program's by a relative error of at most 0.012.
Values may be sent and summed in bfloat16 or wider, within the bound.
A program may use at most 128 MiB of HBM per device.

v0:
```python
import jax
import jax.numpy as jnp
from jax import lax
from jax.sharding import PartitionSpec as P

STEP = 20


beta_one = 0.9
beta_two = 0.95
adam_epsilon = 1e-08


def on_device(gradient, left_basis, first_moment, second_moment):
    basis_panel = lax.all_gather(left_basis, ("tp", "layer"), axis=1, tiled=True)
    rotated = lax.psum_scatter(
        lax.dot_general(
            basis_panel, gradient, (((0,), (0,)), ((), ())), preferred_element_type=jnp.float32
        ).astype(jnp.bfloat16),
        "fsdp",
        scatter_dimension=0,
        tiled=True,
    ).astype(jnp.float32)
    first_new = beta_one * first_moment + (1.0 - beta_one) * rotated
    second_new = beta_two * second_moment + (1.0 - beta_two) * rotated * rotated
    correct_one = 1.0 - beta_one**STEP
    correct_two = 1.0 - beta_two**STEP
    direction = (
        first_new / correct_one / (jnp.sqrt(second_new / correct_two) + adam_epsilon)
    ).astype(jnp.bfloat16)
    gathered = lax.all_gather(direction, "fsdp", axis=0, tiled=True)
    update = jnp.dot(basis_panel, gathered, preferred_element_type=jnp.float32)
    return (update.astype(jnp.bfloat16), first_new, second_new)


def solution(mesh):
    placed = (
        P("fsdp", ("tp", "layer")),
        P("fsdp", ("tp", "layer")),
        P("fsdp", ("tp", "layer")),
        P("fsdp", ("tp", "layer")),
    )
    return jax.shard_map(
        on_device,
        mesh=mesh,
        in_specs=placed,
        out_specs=(
            P("fsdp", ("tp", "layer")),
            P("fsdp", ("tp", "layer")),
            P("fsdp", ("tp", "layer")),
        ),
        check_vma=False,
    )
```

profile of v0, /device:TPU:7, one launch (start us, length us, event | category | flops | bytes accessed | tf_op | source)
XLA Modules:
  0.0 577.2 jit_solution(5299029017668818495)
XLA Ops:
  7.2 0.0 copy-start
  7.2 0.0 all-gather.3.cloned.1.call-start
  7.2 0.7 all-gather.3.cloned.1.call-update
  7.9 0.0 reduce-scatter.2.cloned.1.call-start
  8.0 405.9 %all-gather.3.cloned.1.call-done = bf16[1024,8192]{1,0:T(8,128)(2,1)} async-done(((bf16[1024,256]{1,0:T(8,128)(2,1)}), bf16[1024,8192]{1,0:T(8,128)(2,1)}) %all-gather.3.cloned.1.call-update) | async-done | bytes 16777232 | tf_op jit(solution)/shard_map/all_gather | solution.py:15
  413.8 0.0 copy-done
  413.8 15.5 %convolution_convert_fusion = bf16[8192,448]{0,1:T(8,128)(2,1)} fusion(bf16[1024,448]{0,1:T(8,128)(2,1)S(1)} %copy-done, bf16[1024,8192]{1,0:T(8,128)(2,1)} %all-gather.3.cloned.1.call-done), kind=kOutput, calls=%fused_computation | convolution fusion | flops 7519862784 | bytes 25034752 | tf_op jit(solution)/shard_map/dot_general | solution.py:17
  429.3 0.0 copy-start.1
  429.3 0.0 reduce-scatter.2.cloned.1.call-update
  429.4 0.0 all-gather.5.cloned.1.call-start
  429.4 73.5 %reduce-scatter.2.cloned.1.call-done = bf16[1024,448]{0,1:T(8,128)(2,1)} async-done(((bf16[8192,448]{0,1:T(8,128)(2,1)}), bf16[1024,448]{0,1:T(8,128)(2,1)}) %reduce-scatter.2.cloned.1.call-update) | async-done | bytes 917520 | tf_op jit(solution)/shard_map/reduce_scatter | solution.py:16
  502.9 0.0 copy-done.1
  502.9 4.9 divide_convert_fusion
  507.7 0.0 all-gather.5.cloned.1.call-update
  507.8 48.7 %all-gather.5.cloned.1.call-done = bf16[8192,448]{0,1:T(8,128)(2,1)} async-done(((bf16[1024,448]{0,1:T(8,128)(2,1)}), bf16[8192,448]{0,1:T(8,128)(2,1)}) %all-gather.5.cloned.1.call-update) | async-done | bytes 7340048 | tf_op jit(solution)/shard_map/all_gather | solution.py:31
  556.4 14.2 %fusion.2 = bf16[1024,448]{0,1:T(8,128)(2,1)} fusion(bf16[8192,448]{0,1:T(8,128)(2,1)} %all-gather.5.cloned.1.call-done, bf16[1024,8192]{1,0:T(8,128)(2,1)} %all-gather.3.cloned.1.call-done), kind=kOutput, calls=%fused_computation.7 | convolution fusion | flops 7516651520 | bytes 25034752 | tf_op jit(solution)/shard_map/dot_general | solution.py:32
Async XLA Ops:
  7.2 406.7 %copy-start = (bf16[1024,448]{0,1:T(8,128)(2,1)S(1)}, bf16[1024,448]{0,1:T(8,128)(2,1)}, u32[]{:S(2)}) copy-start(bf16[1024,448]{0,1:T(8,128)(2,1)} %param.4) | copy-start | bytes 2752516
  7.2 406.6 %all-gather.3.cloned.1.call-start = ((), (), s32[]{:S(2)}) async-start(), calls=%async_computation.1 | async-start | bytes 17301504 | tf_op jit(solution)/shard_map/all_gather | solution.py:15
  7.9 495.0 %reduce-scatter.2.cloned.1.call-start = ((), (), s32[]{:S(2)}) async-start(), calls=%async_computation.2 | async-start | bytes 8257536 | tf_op jit(solution)/shard_map/reduce_scatter | solution.py:16
  429.3 73.6 %copy-start.1 = (f32[1024,448]{0,1:T(8,128)S(1)}, f32[1024,448]{0,1:T(8,128)}, u32[]{:S(2)}) copy-start(f32[1024,448]{0,1:T(8,128)} %param.6) | copy-start | bytes 5505028
  429.4 127.1 %all-gather.5.cloned.1.call-start = ((), (), s32[]{:S(2)}) async-start(), calls=%async_computation.3 | async-start | bytes 8257536 | tf_op jit(solution)/shard_map/all_gather | solution.py:31
Sparse Core Ops, SparseCore 0:
  9.7 404.0 all-gather.2
  429.5 73.3 reduce-scatter.1
  507.9 48.4 all-gather.4
where the time goes:
time: 578 us; the launch traced here: 577 us
  waiting for transfers between devices  529 us (92%)
  matrix products  29.7 us (5%)
  between operations  13.8 us (2%)
    all_gather x1, waiting for transfers between devices, on_device(): lax.all_gather(left_basis, ('tp', 'layer'), axis=1, tiled=True)  406 us
    reduce_scatter x1, waiting for transfers between devices, on_device(): lax.psum_scatter(lax.dot_general(basis_panel, gradient, (((0,), (0,)), ((...  73.5 us
    all_gather x1, waiting for transfers between devices, on_device(): gathered = lax.all_gather(direction, 'fsdp', axis=0, tiled=True)  48.7 us
    dot_general x1, matrix products, on_device(): lax.dot_general(basis_panel, gradient, (((0,), (0,)), ((), ())), preferre...  15.5 us
    dot_general x1, matrix products, on_device(): update = jnp.dot(basis_panel, gathered, preferred_element_type=jnp.float32)  14.2 us
  transfers between devices with their start and end apart: 3, of which 3 were waited for; matrix products, arithmetic and copies ran while one was open for 0% of the time, Pallas kernels for 0%

commit v1 on v0

v1 whole, which is shorter than its diff:
```python
import jax
import jax.numpy as jnp
from jax import lax
from jax.experimental import pallas as pl
from jax.experimental.pallas import tpu as pltpu
from jax.sharding import PartitionSpec as P

STEP = 20


beta_one = 0.9
beta_two = 0.95
adam_epsilon = 1e-08
correct_one = 1.0 - beta_one**STEP
correct_two = 1.0 - beta_two**STEP

MESH = pl.DeviceIdType.MESH
BF16 = jnp.bfloat16
F32 = jnp.float32

ROWS, COLS, WIDE = 1024, 448, 256
HALF = COLS // 2
NX, NY, NZ = 4, 4, 8
CHUNKS = NX * NZ

PART_P = 608
SPANS = {
    ("P", "F"): (0, PART_P),
    ("P", "A"): (0, PART_P // 2),
    ("P", "B"): (PART_P // 2, PART_P // 2),
    ("Q", "F"): (PART_P, ROWS - PART_P),
    ("Q", "A"): (PART_P, (ROWS - PART_P) // 2),
    ("Q", "B"): ((PART_P + ROWS) // 2, (ROWS - PART_P) // 2),
}
ORDER = (
    (0, 0), (-1, 0), (1, 0), (0, -1), (0, 1), (-1, -1), (1, -1), (-1, 1), (1, 1), (2, 0), (0, -2), (0, 2), (2, -1), (2, 1), (-1, -2), (1, -2), (-1, 2), (1, 2), (0, -3), (0, 3), (2, -2), (2, 2), (-1, -3), (1, -3), (-1, 3), (1, 3), (0, 4), (2, -3), (2, 3), (-1, 4), (1, 4), (2, 4),
)
ARRIVALS = (
    (),
    (("Q", -1, 0, "F"), ("Q", 1, 0, "F"), ("P", 0, -1, "F"), ("P", 0, 1, "F"), ("P", -1, 0, "F"), ("P", 1, 0, "F"), ("Q", 0, -1, "F"), ("Q", 0, 1, "F"),),
    (),
    (("Q", 2, 0, "A"), ("Q", 2, 0, "B"),),
    (("Q", -1, -1, "F"), ("Q", -1, 1, "F"),),
    (("P", -1, -1, "F"), ("P", 1, -1, "F"), ("Q", 1, -1, "F"), ("Q", 1, 1, "F"),),
    (),
    (("P", -1, 1, "F"), ("P", 1, 1, "F"), ("P", 0, -2, "F"), ("P", 0, 2, "F"),),
    (),
    (("P", 2, 0, "A"), ("P", 2, 0, "B"),),
    (("Q", 0, -2, "F"), ("Q", 0, 2, "F"),),
    (),
    (("P", 2, -1, "A"), ("P", 2, -1, "B"), ("Q", 2, -1, "A"), ("Q", 2, 1, "A"), ("Q", 2, -1, "B"), ("Q", 2, 1, "B"),),
    (("P", 2, 1, "A"), ("P", 2, 1, "B"),),
    (("Q", -1, -2, "F"), ("Q", -1, 2, "F"), ("P", -1, -2, "F"), ("P", 1, -2, "F"),),
    (("Q", 1, -2, "F"), ("Q", 1, 2, "F"),),
    (("P", -1, 2, "F"), ("P", 1, 2, "F"),),
    (),
    (("P", 0, -3, "F"), ("P", 0, 3, "F"), ("P", 2, -2, "A"), ("P", 2, -2, "B"), ("Q", 0, -3, "F"), ("Q", 0, 3, "F"),),
    (("P", 2, 2, "A"), ("P", 2, 2, "B"),),
    (("Q", 2, -2, "A"), ("Q", 2, 2, "A"), ("Q", 2, -2, "B"), ("Q", 2, 2, "B"),),
    (),
    (("P", -1, -3, "F"), ("P", 1, -3, "F"), ("Q", -1, -3, "F"), ("Q", -1, 3, "F"),),
    (("Q", 1, -3, "F"), ("Q", 1, 3, "F"), ("P", -1, 3, "F"), ("P", 1, 3, "F"),),
    (),
    (),
    (("P", 0, 4, "A"), ("P", 0, 4, "B"), ("P", 2, -3, "A"), ("P", 2, -3, "B"), ("Q", 0, 4, "A"), ("Q", 0, 4, "B"),),
    (("P", 2, 3, "A"), ("P", 2, 3, "B"), ("Q", 2, -3, "A"), ("Q", 2, 3, "A"), ("P", -1, 4, "A"), ("P", 1, 4, "A"), ("Q", 2, -3, "B"), ("Q", 2, 3, "B"),),
    (),
    (("Q", -1, 4, "A"), ("Q", -1, 4, "B"), ("P", -1, 4, "B"), ("P", 1, 4, "B"),),
    (("Q", 1, 4, "A"), ("Q", 1, 4, "B"),),
    (("P", 2, 4, "A"), ("Q", 2, 4, "A"), ("Q", 2, 4, "B"), ("P", 2, 4, "B"),),
)
SLOT = {offset: slot for slot, offset in enumerate(ORDER)}

LAG_SUM, LAG_OWN, LAG_PASS, LAG_UPDATE = 1, 5, 8, 10


def bits(values, shift):
    word = sum((((value >> shift) & 1) << k) for k, value in enumerate(values))
    return word - (1 << 32) if word >= 1 << 31 else word


X_BITS = [bits([i % NX for i, _ in ORDER], s) for s in range(2)]
Z_BITS = [bits([j % NZ for _, j in ORDER], s) for s in range(3)]


def lookup(words, t):
    total = 0
    for s, word in enumerate(words):
        total = total + (lax.shift_right_logical(jnp.int32(word), t) & 1) * (1 << s)
    return total


def onward(part, i, j, half):
    out = []
    if part == "P":
        if i == 0:
            if j == 0:
                out += [("z+", "F"), ("z-", "F")]
            elif j in (-1, -2):
                out += [("z+", "F")]
            elif j in (1, 2):
                out += [("z-", "F")]
            elif j == -3:
                out += [("z+", "A")]
            elif j == 3:
                out += [("z-", "B")]
            out += [("x+", half), ("x-", half)]
        elif i == -1 and half in "FA":
            out += [("x+", "A")]
        elif i == 1 and half in "FB":
            out += [("x-", "B")]
    elif j == 0:
        if i == 0:
            out += [("x+", "F"), ("x-", "F")]
        elif i == -1:
            out += [("x+", "A")]
        elif i == 1:
            out += [("x-", "B")]
        out += [("z+", half), ("z-", half)]
    elif j in (-1, -2):
        out += [("z+", half)]
    elif j in (1, 2):
        out += [("z-", half)]
    elif j == -3 and half in "FA":
        out += [("z+", "A")]
    elif j == 3 and half in "FB":
        out += [("z-", "B")]
    return out


def seen_from(link, i, j):
    i += {"x+": -1, "x-": 1}.get(link, 0)
    j += {"z+": -1, "z-": 1}.get(link, 0)
    return (i + 1) % NX - 1, (j + 3) % NZ - 3


def kernel(
    grad_hbm, basis_hbm, first_hbm, second_hbm,
    update_hbm, first_out, second_out,
    panel, grad, grad_t, first, second, own, pair_out, pair_in, sum_out, sum_in, turned, steps, total, update,
    load_sem, store_sem, chunk_sem, chunk_sent, pair_sem, pair_sent, sum_sem, sum_sent, near_sem, far_sem, step_sent,
):
    f, tp, layer = lax.axis_index("fsdp"), lax.axis_index("tp"), lax.axis_index("layer")
    x, y, z, c = layer * 2 + tp // NZ, f // 2, tp % NZ, f % 2

    def place(px, py, pz, pc):
        return (py * 2 + pc, (px % 2) * NZ + pz, px // 2)

    partner = place(x, y, z, 1 - c)
    neighbours = {
        "x+": place((x + 1) % NX, y, z, c),
        "x-": place((x + NX - 1) % NX, y, z, c),
        "z+": place(x, y, (z + 1) % NZ, c),
        "z-": place(x, y, (z + NZ - 1) % NZ, c),
    }

    def remote(source, target, send_sem, recv_sem, device):
        return pltpu.make_async_remote_copy(
            src_ref=source, dst_ref=target, send_sem=send_sem, recv_sem=recv_sem, device_id=device, device_id_type=MESH
        )

    def await_bytes(ref, sem):
        pltpu.make_async_copy(ref, ref, sem).wait()

    loads = [
        pltpu.make_async_copy(basis_hbm, panel.at[0], load_sem.at[0]),
        pltpu.make_async_copy(grad_hbm, grad, load_sem.at[1]),
        pltpu.make_async_copy(first_hbm, first, load_sem.at[2]),
        pltpu.make_async_copy(second_hbm, second, load_sem.at[3]),
    ]
    for load in loads:
        load.start()

    barrier = pltpu.get_barrier_semaphore()
    peers = list(neighbours.values()) + [partner]
    for k in range(1, NY):
        for pc in range(2):
            peers.append(place(x, (y + k) % NY, z, pc))
    for peer in peers:
        pl.semaphore_signal(barrier, inc=1, device_id=peer, device_id_type=MESH)
    loads[0].wait()
    pl.semaphore_wait(barrier, len(peers))

    def chunk_piece(part, half, slot):
        start, size = SPANS[part, half]
        return panel.at[slot, pl.ds(start, size)], chunk_sem.at[slot, 2 * (part == "Q") + (half == "B")]

    def hand_on(part, i, j, link, half):
        start, size = SPANS[part, half]
        target, sem = chunk_piece(part, half, SLOT[seen_from(link, i, j)])
        remote(panel.at[SLOT[i, j], pl.ds(start, size)], target, chunk_sent, sem, neighbours[link]).start()

    for link in ("x+", "x-"):
        hand_on("Q", 0, 0, link, "F")
    for link in ("z+", "z-"):
        hand_on("P", 0, 0, link, "F")
    for link in ("x+", "x-"):
        hand_on("P", 0, 0, link, "F")
    for link in ("z+", "z-"):
        hand_on("Q", 0, 0, link, "F")

    loads[1].wait()
    for k in range(ROWS // 256):
        block = jnp.concatenate(
            [grad[pl.ds(256 * k, 256), :].astype(F32), jnp.zeros((256, 512 - COLS), F32)], axis=1
        ).T.astype(BF16)
        for h in range(2):
            at = pl.multiple_of(jnp.where(c == h, HALF, 0), 16)
            grad_t[pl.ds(at, HALF), pl.ds(256 * k, 256)] = block[HALF * h : HALF * (h + 1)]
    total[...] = jnp.zeros_like(total)
    turned[pl.ds(COLS, 512 - COLS), :] = jnp.zeros((512 - COLS, WIDE), F32)
    loads[2].wait()
    loads[3].wait()

    def owner_of(t):
        xs, zs = lax.rem(x + lookup(X_BITS, t), NX), lax.rem(z + lookup(Z_BITS, t), NZ)
        return 2 * lax.rem(xs, 2) + zs // 4, lax.rem(zs // 2, 2), 2 * lax.rem(zs, 2) + xs // 2

    def first_product(t):
        product = jnp.dot(grad_t[...], panel[t], preferred_element_type=F32)
        pair_out[t] = product[:HALF].astype(BF16)
        remote(pair_out.at[t], pair_in.at[t], pair_sent, pair_sem.at[t], partner).start()
        own[lax.rem(t, 2)] = product[HALF:]

    def chip_sum(t):
        await_bytes(pair_in.at[t], pair_sem.at[t])
        oy, oc, block = owner_of(t)
        mine = (own[lax.rem(t, 2)] + pair_in[t].astype(F32)).astype(BF16)
        here = (oy == y) & (oc == c)

        @pl.when(here)
        def _():
            sum_in[block, 0] = mine

        @pl.when(jnp.logical_not(here))
        def _():
            sum_out[t] = mine
            place_in = 2 * lax.rem(y - oy + NY, NY) + jnp.where(oc == c, 0, 1)
            remote(
                sum_out.at[t], sum_in.at[block, place_in], sum_sent, sum_sem.at[block, place_in], place(x, oy, z, oc)
            ).start()

    def own_step(t):
        oy, oc, block = owner_of(t)

        @pl.when((oy == y) & (oc == c))
        def _():
            for r in range(1, 2 * NY):
                await_bytes(sum_in.at[block, r], sum_sem.at[block, r])
            for e in range(2):
                rotated = sum_in[block, e].astype(F32)
                for k in range(1, NY):
                    rotated = rotated + sum_in[block, 2 * k + e].astype(F32)
                at = pl.multiple_of(HALF * (c if e == 0 else 1 - c), 8)
                turned[pl.ds(at, HALF), :] = rotated
            for k in range(WIDE // 128):
                rows = pl.ds(pl.multiple_of(block * WIDE + 128 * k, 128), 128)
                rotated = turned[:, pl.ds(128 * k, 128)].T[:, :COLS]
                first_new = beta_one * first[rows, :] + (1.0 - beta_one) * rotated
                second_new = beta_two * second[rows, :] + (1.0 - beta_two) * rotated * rotated
                step = first_new / correct_one / (jnp.sqrt(second_new / correct_two) + adam_epsilon)
                first[rows, :] = first_new
                second[rows, :] = second_new
                step = jnp.concatenate([step, jnp.zeros((128, 512 - COLS), F32)], axis=1).T
                steps[t, :, pl.ds(128 * k, 128)] = step[:COLS].astype(BF16)
            for h in range(2):
                half = pl.ds(HALF * h, HALF)
                for k in range(1, NY):
                    remote(
                        steps.at[t, half], steps.at[t, half], step_sent, near_sem.at[t], place(x, lax.rem(y + k, NY), z, h)
                    ).start()
            remote(steps.at[t], steps.at[t], step_sent, near_sem.at[t], partner).start()
            rows = pl.ds(pl.multiple_of(block * WIDE, WIDE), WIDE)
            pltpu.make_async_copy(first.at[rows], first_out.at[rows], store_sem.at[0]).start()
            pltpu.make_async_copy(second.at[rows], second_out.at[rows], store_sem.at[1]).start()

    def pass_step(t):
        oy, _, _ = owner_of(t)

        @pl.when(oy != y)
        def _():
            half = steps.at[t, pl.ds(pl.multiple_of(HALF * c, 16), HALF)]
            await_bytes(half, near_sem.at[t])
            remote(half, half, step_sent, far_sem.at[t], partner).start()

    def second_product(t):
        oy, oc, _ = owner_of(t)

        @pl.when(oy != y)
        def _():
            await_bytes(steps.at[t, pl.ds(0, HALF)], far_sem.at[t])

        @pl.when((oy == y) & (oc != c))
        def _():
            await_bytes(steps.at[t], near_sem.at[t])

        for k in range(ROWS // 256):
            rows = pl.ds(256 * k, 256)
            total[rows, :] += lax.dot_general(
                panel[t, rows], steps[t], (((1,), (1,)), ((), ())), preferred_element_type=F32
            )

    def body(t, carry):
        for group in range(0, CHUNKS, 8):

            @pl.when((t >= group) & (t < group + 8))
            def _():
                for slot in range(group, group + 8):
                    if ARRIVALS[slot]:

                        @pl.when(t == slot)
                        def _():
                            for part, i, j, half in ARRIVALS[slot]:
                                await_bytes(*chunk_piece(part, half, SLOT[i, j]))
                                for link, piece in onward(part, i, j, half):
                                    hand_on(part, i, j, link, piece)

        def stage(lag, work):
            @pl.when((t >= lag) & (t < CHUNKS + lag))
            def _():
                work(t - lag)

        stage(LAG_SUM, chip_sum)
        stage(0, first_product)
        stage(LAG_OWN, own_step)
        stage(LAG_PASS, pass_step)
        stage(LAG_UPDATE, second_product)
        return carry

    lax.fori_loop(0, CHUNKS + LAG_UPDATE, body, 0)

    stores = []
    for k in range(4):
        rows = pl.ds(256 * k, 256)
        update[rows, :] = total[rows, :].astype(BF16)
        stores.append(pltpu.make_async_copy(update.at[rows], update_hbm.at[rows], store_sem.at[2]))
        stores[-1].start()
    await_bytes(panel.at[pl.ds(1, CHUNKS - 1)], chunk_sent)
    await_bytes(pair_out, pair_sent)
    await_bytes(sum_out.at[pl.ds(0, CHUNKS - 4)], sum_sent)
    await_bytes(steps.at[pl.ds(0, CHUNKS - 4)], step_sent)
    await_bytes(first, store_sem.at[0])
    await_bytes(second, store_sem.at[1])
    await_bytes(update, store_sem.at[2])


def on_device(gradient, left_basis, first_moment, second_moment):
    dma = pltpu.SemaphoreType.DMA
    return pl.pallas_call(
        kernel,
        out_shape=(
            jax.ShapeDtypeStruct((ROWS, COLS), BF16),
            jax.ShapeDtypeStruct((ROWS, COLS), F32),
            jax.ShapeDtypeStruct((ROWS, COLS), F32),
        ),
        in_specs=[pl.BlockSpec(memory_space=pl.ANY)] * 4,
        out_specs=tuple([pl.BlockSpec(memory_space=pl.ANY)] * 3),
        scratch_shapes=[
            pltpu.VMEM((CHUNKS, ROWS, WIDE), BF16),
            pltpu.VMEM((ROWS, COLS), BF16),
            pltpu.VMEM((COLS, ROWS), BF16),
            pltpu.VMEM((ROWS, COLS), F32),
            pltpu.VMEM((ROWS, COLS), F32),
            pltpu.VMEM((2, HALF, WIDE), F32),
            pltpu.VMEM((CHUNKS, HALF, WIDE), BF16),
            pltpu.VMEM((CHUNKS, HALF, WIDE), BF16),
            pltpu.VMEM((CHUNKS, HALF, WIDE), BF16),
            pltpu.VMEM((4, 2 * NY, HALF, WIDE), BF16),
            pltpu.VMEM((512, WIDE), F32),
            pltpu.VMEM((CHUNKS, COLS, WIDE), BF16),
            pltpu.VMEM((ROWS, COLS), F32),
            pltpu.VMEM((ROWS, COLS), BF16),
            dma((4,)),
            dma((3,)),
            dma((CHUNKS, 4)),
            dma,
            dma((CHUNKS,)),
            dma,
            dma((4, 2 * NY)),
            dma,
            dma((CHUNKS,)),
            dma((CHUNKS,)),
            dma,
        ],
        compiler_params=pltpu.CompilerParams(
            collective_id=0, has_side_effects=True, vmem_limit_bytes=60 << 20
        ),
        cost_estimate=pl.CostEstimate(flops=4 * 8192 * ROWS * COLS, bytes_accessed=10 << 20, transcendentals=0),
    )(gradient, left_basis, first_moment, second_moment)


def solution(mesh):
    placed = P("fsdp", ("tp", "layer"))
    return jax.shard_map(
        on_device, mesh=mesh, in_specs=(placed,) * 4, out_specs=(placed,) * 3, check_vma=False
    )
```

time: 578 us -> 176 us (0.30)
  the two profiles are of different devices: /device:TPU:7 before, /device:TPU:39 now
where the time goes in v1:
time: 176 us
  Pallas kernels  161 us (91%)
  local copies, waits for them, and re-layouts  14 us (8%)
    pallas_call x1, Pallas kernels, on_device(): pl.pallas_call(kernel, out_shape=(jax.ShapeDtypeStruct((ROWS, COLS), BF16...  161 us
    unnamed x7, local copies, waits for them, and re-layouts  7.07 us
    pallas_call x3, local copies, waits for them, and re-layouts, on_device(): pl.pallas_call(kernel, out_shape=(jax.ShapeDtypeStruct((ROWS, COLS), BF16...  6.89 us

profile of v1, /device:TPU:39, one launch (start us, length us, event | category | flops | bytes accessed | tf_op | source)
XLA Modules:
  0.0 175.8 jit_solution(18397447900200577450)
XLA Ops:
  0.6 0.0 copy-start.1
  0.6 2.4 %copy.7.grad_hbm = bf16[1024,448]{1,0:T(8,128)(2,1)} copy(bf16[1024,448]{0,1:T(8,128)(2,1)} %param.4) | data formatting | bytes 1835008 | tf_op args[0]
  3.0 0.0 copy-done.1
  3.0 1.8 %copy.8.first_hbm = f32[1024,448]{1,0:T(8,128)} copy(f32[1024,448]{0,1:T(8,128)S(1)} %copy-done.1) | data formatting | bytes 3670016 | tf_op args[2]
  4.9 2.8 %copy.9.second_hbm = f32[1024,448]{1,0:T(8,128)} copy(f32[1024,448]{0,1:T(8,128)} %param.7) | data formatting | bytes 3670016 | tf_op args[3]
  7.7 161.2 %shard_map.67 = (bf16[1024,448]{1,0:T(8,128)(2,1)}, f32[1024,448]{1,0:T(8,128)}, f32[1024,448]{1,0:T(8,128)}) custom-call(bf16[1024,448]{1,0:T(8,128)(2,1)} %copy.7.grad_hbm, bf16[1024,256]{1,0:T(8,128)(2,1)} %basis_hbm.1, f32[1024,448]{1,0:T(8,128)} %copy.8.first_hbm, f32[1024,448]{1,0:T(8,128)} %copy.9.second_hbm), custom_call_target="tpu_custom_call" | custom-call | flops 15032385536 | bytes 10485760 | tf_op jit(solution)/shard_map/pallas_call | solution.py:349
  168.9 2.2 %copy.10 = bf16[1024,448]{0,1:T(8,128)(2,1)} copy(bf16[1024,448]{1,0:T(8,128)(2,1)} %get-tuple-element.3) | data formatting | bytes 1835008 | tf_op jit(solution)/shard_map/pallas_call | solution.py:349
  171.2 0.0 copy-start
  171.2 2.9 %copy.11 = f32[1024,448]{0,1:T(8,128)} copy(f32[1024,448]{1,0:T(8,128)} %get-tuple-element.4) | data formatting | bytes 3670016 | tf_op jit(solution)/shard_map/pallas_call | solution.py:349
  174.1 0.0 copy-done
  174.1 1.7 copy.12
Async XLA Ops:
  0.6 2.4 %copy-start.1 = (f32[1024,448]{0,1:T(8,128)S(1)}, f32[1024,448]{0,1:T(8,128)}, u32[]{:S(2)}) copy-start(f32[1024,448]{0,1:T(8,128)} %param.6) | copy-start | bytes 5505028
  171.2 3.0 %copy-start = (f32[1024,448]{1,0:T(8,128)S(1)}, f32[1024,448]{1,0:T(8,128)}, u32[]{:S(2)}) copy-start(f32[1024,448]{1,0:T(8,128)} %get-tuple-element.5) | copy-start | bytes 5505028

commit v2 on v1

--- a/solution.py
+++ b/solution.py
@@ -20,6 +20,7 @@
 
 ROWS, COLS, WIDE = 1024, 448, 256
 HALF = COLS // 2
+QUARTER = HALF // 2
 NX, NY, NZ = 4, 4, 8
 CHUNKS = NX * NZ
 
@@ -71,7 +72,7 @@
 )
 SLOT = {offset: slot for slot, offset in enumerate(ORDER)}
 
-LAG_SUM, LAG_OWN, LAG_PASS, LAG_UPDATE = 1, 5, 8, 10
+LAG_SUM, LAG_RELAY, LAG_OWN, LAG_PASS, LAG_FAR, LAG_UPDATE = 1, 4, 8, 11, 14, 16
 
 
 def bits(values, shift):
@@ -137,8 +138,8 @@
 def kernel(
     grad_hbm, basis_hbm, first_hbm, second_hbm,
     update_hbm, first_out, second_out,
-    panel, grad, grad_t, first, second, own, pair_out, pair_in, sum_out, sum_in, turned, steps, total, update,
-    load_sem, store_sem, chunk_sem, chunk_sent, pair_sem, pair_sent, sum_sem, sum_sent, near_sem, far_sem, step_sent,
+    panel, grad, grad_t, first, second, own, pair_out, pair_in, sum_out, relay_in, sum_in, steps, total, update,
+    load_sem, store_sem, chunk_sem, chunk_sent, pair_sem, pair_sent, relay_sem, sum_sem, sum_sent, near_sem, quarter_sem, other_sem, step_sent,
 ):
     f, tp, layer = lax.axis_index("fsdp"), lax.axis_index("tp"), lax.axis_index("layer")
     x, y, z, c = layer * 2 + tp // NZ, f // 2, tp % NZ, f % 2
@@ -200,15 +201,10 @@
         hand_on("Q", 0, 0, link, "F")
 
     loads[1].wait()
-    for k in range(ROWS // 256):
-        block = jnp.concatenate(
-            [grad[pl.ds(256 * k, 256), :].astype(F32), jnp.zeros((256, 512 - COLS), F32)], axis=1
-        ).T.astype(BF16)
-        for h in range(2):
-            at = pl.multiple_of(jnp.where(c == h, HALF, 0), 16)
-            grad_t[pl.ds(at, HALF), pl.ds(256 * k, 256)] = block[HALF * h : HALF * (h + 1)]
+    for h in range(2):
+        at = pl.multiple_of(jnp.where(c == h, HALF, 0), 16)
+        grad_t[pl.ds(at, HALF), :] = grad[pl.ds(HALF * h, HALF), :]
     total[...] = jnp.zeros_like(total)
-    turned[pl.ds(COLS, 512 - COLS), :] = jnp.zeros((512 - COLS, WIDE), F32)
     loads[2].wait()
     loads[3].wait()
 
@@ -222,11 +218,16 @@
         remote(pair_out.at[t], pair_in.at[t], pair_sent, pair_sem.at[t], partner).start()
         own[lax.rem(t, 2)] = product[HALF:]
 
+    def quarter(ref, q):
+        return ref.at[pl.ds(pl.multiple_of(QUARTER * q, 16), QUARTER)]
+
     def chip_sum(t):
         await_bytes(pair_in.at[t], pair_sem.at[t])
         oy, oc, block = owner_of(t)
         mine = (own[lax.rem(t, 2)] + pair_in[t].astype(F32)).astype(BF16)
-        here = (oy == y) & (oc == c)
+        away = lax.rem(y - oy + NY, NY)
+        here = (away == 0) & (oc == c)
+        owner = place(x, oy, z, oc)
 
         @pl.when(here)
         def _():
@@ -235,60 +236,102 @@
         @pl.when(jnp.logical_not(here))
         def _():
             sum_out[t] = mine
-            place_in = 2 * lax.rem(y - oy + NY, NY) + jnp.where(oc == c, 0, 1)
-            remote(
-                sum_out.at[t], sum_in.at[block, place_in], sum_sent, sum_sem.at[block, place_in], place(x, oy, z, oc)
-            ).start()
+
+        @pl.when((away == 0) & (oc != c))
+        def _():
+            remote(sum_out.at[t], sum_in.at[block, 1], sum_sent, sum_sem.at[block, 1, 0], owner).start()
+
+        @pl.when(away == 2)
+        def _():
+            for q, step in enumerate((-1, 1)):
+                remote(
+                    quarter(sum_out.at[t], q), relay_in.at[t], sum_sent, relay_sem.at[t],
+                    place(x, lax.rem(y + step + NY, NY), z, c),
+                ).start()
+
+        @pl.when(lax.rem(away, 2) == 1)
+        def _():
+            add_to_owner(t, 1 - away // 2)
+
+    def add_to_owner(t, q):
+        oy, oc, block = owner_of(t)
+        away = lax.rem(y - oy + NY, NY)
+        spot = 2 + 2 * (away // 2) + jnp.where(oc == c, 0, 1)
+        remote(
+            quarter(sum_out.at[t], q), quarter(sum_in.at[block, spot], q), sum_sent, sum_sem.at[block, spot, q],
+            place(x, oy, z, oc),
+        ).start()
+
+    def relay_sum(t):
+        oy, _, _ = owner_of(t)
+        away = lax.rem(y - oy + NY, NY)
+
+        @pl.when(lax.rem(away, 2) == 1)
+        def _():
+            await_bytes(relay_in.at[t], relay_sem.at[t])
+            rows = pl.ds(pl.multiple_of(QUARTER * (away // 2), 16), QUARTER)
+            sum_out[t, rows, :] = (sum_out[t, rows, :].astype(F32) + relay_in[t].astype(F32)).astype(BF16)
+            add_to_owner(t, away // 2)
 
     def own_step(t):
         oy, oc, block = owner_of(t)
 
         @pl.when((oy == y) & (oc == c))
         def _():
-            for r in range(1, 2 * NY):
-                await_bytes(sum_in.at[block, r], sum_sem.at[block, r])
+            await_bytes(sum_in.at[block, 1], sum_sem.at[block, 1, 0])
+            for spot in range(2, 6):
+                for q in range(2):
+                    await_bytes(quarter(sum_in.at[block, spot], q), sum_sem.at[block, spot, q])
+            columns = pl.ds(pl.multiple_of(block * WIDE, WIDE), WIDE)
             for e in range(2):
+                rows = pl.ds(pl.multiple_of(HALF * (c if e == 0 else 1 - c), 16), HALF)
                 rotated = sum_in[block, e].astype(F32)
-                for k in range(1, NY):
-                    rotated = rotated + sum_in[block, 2 * k + e].astype(F32)
-                at = pl.multiple_of(HALF * (c if e == 0 else 1 - c), 8)
-                turned[pl.ds(at, HALF), :] = rotated
-            for k in range(WIDE // 128):
-                rows = pl.ds(pl.multiple_of(block * WIDE + 128 * k, 128), 128)
-                rotated = turned[:, pl.ds(128 * k, 128)].T[:, :COLS]
-                first_new = beta_one * first[rows, :] + (1.0 - beta_one) * rotated
-                second_new = beta_two * second[rows, :] + (1.0 - beta_two) * rotated * rotated
+                for side in range(2):
+                    rotated = rotated + sum_in[block, 2 + 2 * side + e].astype(F32)
+                first_new = beta_one * first[rows, columns] + (1.0 - beta_one) * rotated
+                second_new = beta_two * second[rows, columns] + (1.0 - beta_two) * rotated * rotated
                 step = first_new / correct_one / (jnp.sqrt(second_new / correct_two) + adam_epsilon)
-                first[rows, :] = first_new
-                second[rows, :] = second_new
-                step = jnp.concatenate([step, jnp.zeros((128, 512 - COLS), F32)], axis=1).T
-                steps[t, :, pl.ds(128 * k, 128)] = step[:COLS].astype(BF16)
+                first[rows, columns] = first_new
+                second[rows, columns] = second_new
+                steps[t, rows, :] = step.astype(BF16)
             for h in range(2):
-                half = pl.ds(HALF * h, HALF)
-                for k in range(1, NY):
-                    remote(
-                        steps.at[t, half], steps.at[t, half], step_sent, near_sem.at[t], place(x, lax.rem(y + k, NY), z, h)
-                    ).start()
+                half = steps.at[t, pl.ds(HALF * h, HALF)]
+                for k in (1, NY - 1):
+                    remote(half, half, step_sent, near_sem.at[t], place(x, lax.rem(y + k, NY), z, h)).start()
             remote(steps.at[t], steps.at[t], step_sent, near_sem.at[t], partner).start()
-            rows = pl.ds(pl.multiple_of(block * WIDE, WIDE), WIDE)
-            pltpu.make_async_copy(first.at[rows], first_out.at[rows], store_sem.at[0]).start()
-            pltpu.make_async_copy(second.at[rows], second_out.at[rows], store_sem.at[1]).start()
+            pltpu.make_async_copy(first.at[:, columns], first_out.at[:, columns], store_sem.at[0]).start()
+            pltpu.make_async_copy(second.at[:, columns], second_out.at[:, columns], store_sem.at[1]).start()
+
+    def my_half(t):
+        return steps.at[t, pl.ds(pl.multiple_of(HALF * c, 16), HALF)]
 
     def pass_step(t):
         oy, _, _ = owner_of(t)
-
-        @pl.when(oy != y)
-        def _():
-            half = steps.at[t, pl.ds(pl.multiple_of(HALF * c, 16), HALF)]
-            await_bytes(half, near_sem.at[t])
-            remote(half, half, step_sent, far_sem.at[t], partner).start()
+        away = lax.rem(y - oy + NY, NY)
+
+        @pl.when(lax.rem(away, 2) == 1)
+        def _():
+            await_bytes(my_half(t), near_sem.at[t])
+            q = away // 2
+            part = quarter(my_half(t), q)
+            remote(part, part, step_sent, quarter_sem.at[t, q], place(x, lax.rem(y + 1 + 2 * q, NY), z, c)).start()
+            remote(my_half(t), my_half(t), step_sent, other_sem.at[t], partner).start()
+
+    def pass_far(t):
+        oy, _, _ = owner_of(t)
+
+        @pl.when(lax.rem(y - oy + NY, NY) == 2)
+        def _():
+            for q in range(2):
+                await_bytes(quarter(my_half(t), q), quarter_sem.at[t, q])
+            remote(my_half(t), my_half(t), step_sent, other_sem.at[t], partner).start()
 
     def second_product(t):
         oy, oc, _ = owner_of(t)
 
         @pl.when(oy != y)
         def _():
-            await_bytes(steps.at[t, pl.ds(0, HALF)], far_sem.at[t])
+            await_bytes(steps.at[t, pl.ds(0, HALF)], other_sem.at[t])
 
         @pl.when((oy == y) & (oc != c))
         def _():
@@ -296,8 +339,8 @@
 
         for k in range(ROWS // 256):
             rows = pl.ds(256 * k, 256)
-            total[rows, :] += lax.dot_general(
-                panel[t, rows], steps[t], (((1,), (1,)), ((), ())), preferred_element_type=F32
+            total[:, rows] += lax.dot_general(
+                steps[t], panel[t, rows], (((1,), (1,)), ((), ())), preferred_element_type=F32
             )
 
     def body(t, carry):
@@ -322,8 +365,10 @@
 
         stage(LAG_SUM, chip_sum)
         stage(0, first_product)
+        stage(LAG_RELAY, relay_sum)
         stage(LAG_OWN, own_step)
         stage(LAG_PASS, pass_step)
+        stage(LAG_FAR, pass_far)
         stage(LAG_UPDATE, second_product)
         return carry
 
@@ -332,8 +377,8 @@
     stores = []
     for k in range(4):
         rows = pl.ds(256 * k, 256)
-        update[rows, :] = total[rows, :].astype(BF16)
-        stores.append(pltpu.make_async_copy(update.at[rows], update_hbm.at[rows], store_sem.at[2]))
+        update[:, rows] = total[:, rows].astype(BF16)
+        stores.append(pltpu.make_async_copy(update.at[:, rows], update_hbm.at[:, rows], store_sem.at[2]))
         stores[-1].start()
     await_bytes(panel.at[pl.ds(1, CHUNKS - 1)], chunk_sent)
     await_bytes(pair_out, pair_sent)
@@ -346,39 +391,41 @@
 
 def on_device(gradient, left_basis, first_moment, second_moment):
     dma = pltpu.SemaphoreType.DMA
-    return pl.pallas_call(
+    outs = pl.pallas_call(
         kernel,
         out_shape=(
-            jax.ShapeDtypeStruct((ROWS, COLS), BF16),
-            jax.ShapeDtypeStruct((ROWS, COLS), F32),
-            jax.ShapeDtypeStruct((ROWS, COLS), F32),
+            jax.ShapeDtypeStruct((COLS, ROWS), BF16),
+            jax.ShapeDtypeStruct((COLS, ROWS), F32),
+            jax.ShapeDtypeStruct((COLS, ROWS), F32),
         ),
         in_specs=[pl.BlockSpec(memory_space=pl.ANY)] * 4,
         out_specs=tuple([pl.BlockSpec(memory_space=pl.ANY)] * 3),
         scratch_shapes=[
             pltpu.VMEM((CHUNKS, ROWS, WIDE), BF16),
-            pltpu.VMEM((ROWS, COLS), BF16),
             pltpu.VMEM((COLS, ROWS), BF16),
-            pltpu.VMEM((ROWS, COLS), F32),
-            pltpu.VMEM((ROWS, COLS), F32),
+            pltpu.VMEM((COLS, ROWS), BF16),
+            pltpu.VMEM((COLS, ROWS), F32),
+            pltpu.VMEM((COLS, ROWS), F32),
             pltpu.VMEM((2, HALF, WIDE), F32),
             pltpu.VMEM((CHUNKS, HALF, WIDE), BF16),
             pltpu.VMEM((CHUNKS, HALF, WIDE), BF16),
             pltpu.VMEM((CHUNKS, HALF, WIDE), BF16),
-            pltpu.VMEM((4, 2 * NY, HALF, WIDE), BF16),
-            pltpu.VMEM((512, WIDE), F32),
+            pltpu.VMEM((CHUNKS, QUARTER, WIDE), BF16),
+            pltpu.VMEM((4, 6, HALF, WIDE), BF16),
             pltpu.VMEM((CHUNKS, COLS, WIDE), BF16),
-            pltpu.VMEM((ROWS, COLS), F32),
-            pltpu.VMEM((ROWS, COLS), BF16),
+            pltpu.VMEM((COLS, ROWS), F32),
+            pltpu.VMEM((COLS, ROWS), BF16),
             dma((4,)),
             dma((3,)),
             dma((CHUNKS, 4)),
             dma,
             dma((CHUNKS,)),
             dma,
-            dma((4, 2 * NY)),
+            dma((CHUNKS,)),
+            dma((4, 6, 2)),
             dma,
             dma((CHUNKS,)),
+            dma((CHUNKS, 2)),
             dma((CHUNKS,)),
             dma,
         ],
@@ -386,7 +433,8 @@
             collective_id=0, has_side_effects=True, vmem_limit_bytes=60 << 20
         ),
         cost_estimate=pl.CostEstimate(flops=4 * 8192 * ROWS * COLS, bytes_accessed=10 << 20, transcendentals=0),
-    )(gradient, left_basis, first_moment, second_moment)
+    )(gradient.T, left_basis, first_moment.T, second_moment.T)
+    return tuple(out.T for out in outs)
 
 
 def solution(mesh):

time: 176 us -> 137 us (0.78)
  the two profiles are of different devices: /device:TPU:39 before, /device:TPU:7 now
where the time goes in v2:
time: 137 us
  Pallas kernels  131 us (96%)
  local copies, waits for them, and re-layouts  5.69 us (4%)
    pallas_call x1, Pallas kernels, on_device(): pl.pallas_call(kernel, out_shape=(jax.ShapeDtypeStruct((COLS, ROWS), BF16...  131 us
    unnamed x7, local copies, waits for them, and re-layouts  5.69 us

profile of v2, /device:TPU:7, one launch (start us, length us, event | category | flops | bytes accessed | tf_op | source)
XLA Modules:
  0.0 136.8 jit_solution(5102450319342198893)
XLA Ops:
  0.6 130.5 %shard_map.67 = (bf16[448,1024]{1,0:T(8,128)(2,1)}, f32[448,1024]{1,0:T(8,128)}, f32[448,1024]{1,0:T(8,128)}) custom-call(bf16[448,1024]{1,0:T(8,128)(2,1)} %bitcast.11, bf16[1024,256]{1,0:T(8,128)(2,1)} %basis_hbm.1, f32[448,1024]{1,0:T(8,128)} %bitcast.9, f32[448,1024]{1,0:T(8,128)} %bitcast.10), custom_call_target="tpu_custom_call" | custom-call | flops 15032385536 | bytes 10485760 | tf_op jit(solution)/shard_map/pallas_call | solution.py:394
  131.2 0.0 copy-start.1
  131.2 2.3 %copy.10 = bf16[1024,448]{0,1:T(8,128)(2,1)} copy(bf16[1024,448]{0,1:T(8,128)(2,1)} %bitcast.8) | data formatting | bytes 1835008
  133.5 0.0 copy-done.1
  133.5 0.0 copy-start
  133.5 1.2 copy.11
  134.7 0.9 copy-done
  135.6 1.2 copy.12
Async XLA Ops:
  131.2 2.3 %copy-start.1 = (f32[448,1024]{1,0:T(8,128)S(1)}, f32[448,1024]{1,0:T(8,128)}, u32[]{:S(2)}) copy-start(f32[448,1024]{1,0:T(8,128)} %get-tuple-element.7) | copy-start | bytes 5505028
  133.5 2.2 %copy-start = (f32[448,1024]{1,0:T(8,128)S(1)}, f32[448,1024]{1,0:T(8,128)}, u32[]{:S(2)}) copy-start(f32[448,1024]{1,0:T(8,128)} %get-tuple-element.8) | copy-start | bytes 5505028

commit v3 on v2

--- a/solution.py
+++ b/solution.py
@@ -39,40 +39,40 @@
 ARRIVALS = (
     (),
     (("Q", -1, 0, "F"), ("Q", 1, 0, "F"), ("P", 0, -1, "F"), ("P", 0, 1, "F"), ("P", -1, 0, "F"), ("P", 1, 0, "F"), ("Q", 0, -1, "F"), ("Q", 0, 1, "F"),),
-    (),
     (("Q", 2, 0, "A"), ("Q", 2, 0, "B"),),
     (("Q", -1, -1, "F"), ("Q", -1, 1, "F"),),
+    (),
     (("P", -1, -1, "F"), ("P", 1, -1, "F"), ("Q", 1, -1, "F"), ("Q", 1, 1, "F"),),
     (),
     (("P", -1, 1, "F"), ("P", 1, 1, "F"), ("P", 0, -2, "F"), ("P", 0, 2, "F"),),
     (),
-    (("P", 2, 0, "A"), ("P", 2, 0, "B"),),
-    (("Q", 0, -2, "F"), ("Q", 0, 2, "F"),),
-    (),
-    (("P", 2, -1, "A"), ("P", 2, -1, "B"), ("Q", 2, -1, "A"), ("Q", 2, 1, "A"), ("Q", 2, -1, "B"), ("Q", 2, 1, "B"),),
-    (("P", 2, 1, "A"), ("P", 2, 1, "B"),),
-    (("Q", -1, -2, "F"), ("Q", -1, 2, "F"), ("P", -1, -2, "F"), ("P", 1, -2, "F"),),
+    (("P", 2, 0, "A"), ("P", 2, 0, "B"), ("Q", 0, -2, "F"), ("Q", 0, 2, "F"),),
+    (("P", 2, -1, "A"), ("P", 2, -1, "B"), ("Q", 2, -1, "A"), ("Q", 2, 1, "A"),),
+    (("Q", 2, -1, "B"), ("Q", 2, 1, "B"), ("P", 2, 1, "A"), ("P", 2, 1, "B"),),
+    (),
+    (("Q", -1, -2, "F"), ("Q", -1, 2, "F"),),
+    (("P", -1, -2, "F"), ("P", 1, -2, "F"),),
     (("Q", 1, -2, "F"), ("Q", 1, 2, "F"),),
     (("P", -1, 2, "F"), ("P", 1, 2, "F"),),
-    (),
-    (("P", 0, -3, "F"), ("P", 0, 3, "F"), ("P", 2, -2, "A"), ("P", 2, -2, "B"), ("Q", 0, -3, "F"), ("Q", 0, 3, "F"),),
-    (("P", 2, 2, "A"), ("P", 2, 2, "B"),),
-    (("Q", 2, -2, "A"), ("Q", 2, 2, "A"), ("Q", 2, -2, "B"), ("Q", 2, 2, "B"),),
-    (),
-    (("P", -1, -3, "F"), ("P", 1, -3, "F"), ("Q", -1, -3, "F"), ("Q", -1, 3, "F"),),
+    (("P", 0, -3, "F"), ("P", 0, 3, "F"),),
+    (("P", 2, -2, "A"), ("P", 2, -2, "B"), ("Q", 0, -3, "F"), ("Q", 0, 3, "F"),),
+    (("P", 2, 2, "A"), ("P", 2, 2, "B"), ("Q", 2, -2, "A"), ("Q", 2, 2, "A"),),
+    (("Q", 2, -2, "B"), ("Q", 2, 2, "B"),),
+    (("P", -1, -3, "F"), ("P", 1, -3, "F"),),
+    (("Q", -1, -3, "F"), ("Q", -1, 3, "F"),),
     (("Q", 1, -3, "F"), ("Q", 1, 3, "F"), ("P", -1, 3, "F"), ("P", 1, 3, "F"),),
     (),
-    (),
-    (("P", 0, 4, "A"), ("P", 0, 4, "B"), ("P", 2, -3, "A"), ("P", 2, -3, "B"), ("Q", 0, 4, "A"), ("Q", 0, 4, "B"),),
-    (("P", 2, 3, "A"), ("P", 2, 3, "B"), ("Q", 2, -3, "A"), ("Q", 2, 3, "A"), ("P", -1, 4, "A"), ("P", 1, 4, "A"), ("Q", 2, -3, "B"), ("Q", 2, 3, "B"),),
-    (),
-    (("Q", -1, 4, "A"), ("Q", -1, 4, "B"), ("P", -1, 4, "B"), ("P", 1, 4, "B"),),
-    (("Q", 1, 4, "A"), ("Q", 1, 4, "B"),),
-    (("P", 2, 4, "A"), ("Q", 2, 4, "A"), ("Q", 2, 4, "B"), ("P", 2, 4, "B"),),
+    (("P", 0, 4, "A"), ("P", 0, 4, "B"), ("P", 2, -3, "A"), ("P", 2, -3, "B"),),
+    (("Q", 0, 4, "A"), ("Q", 0, 4, "B"), ("P", 2, 3, "A"), ("P", 2, 3, "B"),),
+    (("Q", 2, -3, "A"), ("Q", 2, 3, "A"), ("Q", 2, -3, "B"), ("Q", 2, 3, "B"), ("P", -1, 4, "A"), ("P", 1, 4, "A"),),
+    (("Q", -1, 4, "A"), ("Q", -1, 4, "B"),),
+    (("P", -1, 4, "B"), ("P", 1, 4, "B"), ("Q", 1, 4, "A"), ("Q", 1, 4, "B"),),
+    (("P", 2, 4, "A"), ("Q", 2, 4, "A"), ("Q", 2, 4, "B"),),
+    (("P", 2, 4, "B"),),
 )
 SLOT = {offset: slot for slot, offset in enumerate(ORDER)}
 
-LAG_SUM, LAG_RELAY, LAG_OWN, LAG_PASS, LAG_FAR, LAG_UPDATE = 1, 4, 8, 11, 14, 16
+LAG_SUM, LAG_RELAY, LAG_OWN, LAG_PASS, LAG_FAR, LAG_UPDATE = 1, 3, 7, 10, 13, 15
 
 
 def bits(values, shift):

time: 137 us -> 135 us (0.985)
  Pallas kernels: 131 us -> 128 us
    pallas_call x1, Pallas kernels: 131 us -> 128 us  [on_device(): pl.pallas_call(kernel, out_shape=(jax.ShapeDtypeStruct((COLS, ROWS), BF16...]
where the time goes in v3:
time: 135 us
  Pallas kernels  128 us (95%)
  local copies, waits for them, and re-layouts  5.69 us (4%)
    pallas_call x1, Pallas kernels, on_device(): pl.pallas_call(kernel, out_shape=(jax.ShapeDtypeStruct((COLS, ROWS), BF16...  128 us
    unnamed x7, local copies, waits for them, and re-layouts  5.69 us

profile of v3, /device:TPU:7, one launch (start us, length us, event | category | flops | bytes accessed | tf_op | source)
XLA Modules:
  0.0 134.8 jit_solution(16381139432433873979)
XLA Ops:
  0.6 128.4 %shard_map.67 = (bf16[448,1024]{1,0:T(8,128)(2,1)}, f32[448,1024]{1,0:T(8,128)}, f32[448,1024]{1,0:T(8,128)}) custom-call(bf16[448,1024]{1,0:T(8,128)(2,1)} %bitcast.11, bf16[1024,256]{1,0:T(8,128)(2,1)} %basis_hbm.1, f32[448,1024]{1,0:T(8,128)} %bitcast.9, f32[448,1024]{1,0:T(8,128)} %bitcast.10), custom_call_target="tpu_custom_call" | custom-call | flops 15032385536 | bytes 10485760 | tf_op jit(solution)/shard_map/pallas_call | solution.py:394
  129.1 0.0 copy-start.1
  129.1 2.3 %copy.10 = bf16[1024,448]{0,1:T(8,128)(2,1)} copy(bf16[1024,448]{0,1:T(8,128)(2,1)} %bitcast.8) | data formatting | bytes 1835008
  131.4 0.0 copy-done.1
  131.4 0.0 copy-start
  131.4 1.2 copy.11
  132.6 0.9 copy-done
  133.5 1.2 copy.12
Async XLA Ops:
  129.1 2.3 %copy-start.1 = (f32[448,1024]{1,0:T(8,128)S(1)}, f32[448,1024]{1,0:T(8,128)}, u32[]{:S(2)}) copy-start(f32[448,1024]{1,0:T(8,128)} %get-tuple-element.7) | copy-start | bytes 5505028
  131.4 2.2 %copy-start = (f32[448,1024]{1,0:T(8,128)S(1)}, f32[448,1024]{1,0:T(8,128)}, u32[]{:S(2)}) copy-start(f32[448,1024]{1,0:T(8,128)} %get-tuple-element.8) | copy-start | bytes 5505028

commit v4 on v3

--- a/solution.py
+++ b/solution.py
@@ -363,8 +363,8 @@
             def _():
                 work(t - lag)
 
+        stage(0, first_product)
         stage(LAG_SUM, chip_sum)
-        stage(0, first_product)
         stage(LAG_RELAY, relay_sum)
         stage(LAG_OWN, own_step)
         stage(LAG_PASS, pass_step)

time: 135 us -> 135 us (level)
  no operation moved by 1% of the time
where the time goes in v4:
time: 135 us; the launch traced here: 134 us
  Pallas kernels  128 us (95%)
  local copies, waits for them, and re-layouts  5.69 us (4%)
    pallas_call x1, Pallas kernels, on_device(): pl.pallas_call(kernel, out_shape=(jax.ShapeDtypeStruct((COLS, ROWS), BF16...  128 us
    unnamed x7, local copies, waits for them, and re-layouts  5.69 us

profile of v4, /device:TPU:7, one launch (start us, length us, event | category | flops | bytes accessed | tf_op | source)
XLA Modules:
  0.0 134.4 jit_solution(5737337849015078635)
XLA Ops:
  0.6 128.0 %shard_map.67 = (bf16[448,1024]{1,0:T(8,128)(2,1)}, f32[448,1024]{1,0:T(8,128)}, f32[448,1024]{1,0:T(8,128)}) custom-call(bf16[448,1024]{1,0:T(8,128)(2,1)} %bitcast.11, bf16[1024,256]{1,0:T(8,128)(2,1)} %basis_hbm.1, f32[448,1024]{1,0:T(8,128)} %bitcast.9, f32[448,1024]{1,0:T(8,128)} %bitcast.10), custom_call_target="tpu_custom_call" | custom-call | flops 15032385536 | bytes 10485760 | tf_op jit(solution)/shard_map/pallas_call | solution.py:394
  128.7 0.0 copy-start.1
  128.7 2.3 %copy.10 = bf16[1024,448]{0,1:T(8,128)(2,1)} copy(bf16[1024,448]{0,1:T(8,128)(2,1)} %bitcast.8) | data formatting | bytes 1835008
  131.0 0.0 copy-done.1
  131.0 0.0 copy-start
  131.0 1.2 copy.11
  132.2 0.9 copy-done
  133.2 1.2 copy.12
Async XLA Ops:
  128.7 2.3 %copy-start.1 = (f32[448,1024]{1,0:T(8,128)S(1)}, f32[448,1024]{1,0:T(8,128)}, u32[]{:S(2)}) copy-start(f32[448,1024]{1,0:T(8,128)} %get-tuple-element.7) | copy-start | bytes 5505028
  131.0 2.2 %copy-start = (f32[448,1024]{1,0:T(8,128)S(1)}, f32[448,1024]{1,0:T(8,128)}, u32[]{:S(2)}) copy-start(f32[448,1024]{1,0:T(8,128)} %get-tuple-element.8) | copy-start | bytes 5505028
